TPU v7x, 32 devices: a whole 2x2x4 slice. The times are simulated.
32 devices in a mesh: dp: 8 (over y, x, core), head: 4 (over z).
Axes of the slice: x: 2, y: 2, z: 4, core: 2. Of those that a mesh axis runs over, the one named last changes fastest.
Arguments:
- tokens: bfloat16 [16384, 768], P(('dp', 'head')), may hold values from -6 to 6
- cotangent: float32 [16384, 768], P(('dp', 'head')), may hold values from -6 to 6
- lengths: int32 [16], P('dp'), may hold values from 128 to 1920, as said below
- qkv_master: float32 [768, 2304], P('dp'), may hold values from -0.21875 to 0.21875
- out_master: float32 [768, 768], P('dp'), may hold values from -6 to 6
- up_master: float32 [768, 3072], P('dp'), may hold values from -0.21875 to 0.21875
- down_master: float32 [3072, 768], P('dp'), may hold values from -0.109375 to 0.109375
- vector_master: float32 [13, 768], replicated, may hold values from -0.9 to 1.6
- qkv_first: float32 [768, 2304], P('dp'), may hold values from -24 to 24
- qkv_second: float32 [768, 2304], P('dp'), may hold values from 1.47456 to 5.89824
- out_first: float32 [768, 768], P('dp'), may hold values from -4 to 4
- out_second: float32 [768, 768], P('dp'), may hold values from 0.01024 to 0.04096
- up_first: float32 [768, 3072], P('dp'), may hold values from -16 to 16
- up_second: float32 [768, 3072], P('dp'), may hold values from 0.65536 to 2.62144
- down_first: float32 [3072, 768], P('dp'), may hold values from -32 to 32
- down_second: float32 [3072, 768], P('dp'), may hold values from 2.62144 to 10.48576
- vector_first: float32 [13, 768], replicated, may hold values from -40 to 40
- vector_second: float32 [13, 768], replicated, may hold values from 4.096 to 16.384
Outputs:
- output: bfloat16 [16384, 768], P(('dp', 'head'))
- input_grad: float32 [16384, 768], P(('dp', 'head'))
- qkv_first_new: float32 [768, 2304], P('dp')
- qkv_second_new: float32 [768, 2304], P('dp')
- qkv_master_new: float32 [768, 2304], P('dp')
- out_first_new: float32 [768, 768], P('dp')
- out_second_new: float32 [768, 768], P('dp')
- out_master_new: float32 [768, 768], P('dp')
- up_first_new: float32 [768, 3072], P('dp')
- up_second_new: float32 [768, 3072], P('dp')
- up_master_new: float32 [768, 3072], P('dp')
- down_first_new: float32 [3072, 768], P('dp')
- down_second_new: float32 [3072, 768], P('dp')
- down_master_new: float32 [3072, 768], P('dp')
- vector_first_new: float32 [13, 768], replicated
- vector_second_new: float32 [13, 768], replicated
- vector_master_new: float32 [13, 768], replicated
Inputs may be any that keep to these rules, and one draw needn't show every extreme that they name: `lengths`: each group of 2048 tokens holds 2 sequences in the order given; a sequence takes its length rounded up to a multiple of 64 rows, and these rows fill the group exactly; rows past a sequence's length are padding.
All inputs are finite; a program needn't handle non-finite values.
Results may differ from a plain program's by a relative error of at most 0.02.
Values may be sent and summed in bfloat16 or wider, within the bound.
A program may use at most 256 MiB of HBM per device.

v0:
```python
import math

import jax
import jax.numpy as jnp
from jax import lax
from jax.sharding import PartitionSpec as P

D = 768
H = 12
HD = 64
FF = 3072
SPAN = 64
STEP = 10
OUT_FAN = 1


highest = lax.Precision.HIGHEST
norm_epsilon = 1e-05
first_decay = 0.9
second_decay = 0.999
adam_epsilon = 1e-08
weight_decay = 0.01
vector_rate = 0.2


def layer_norm(residual, gain_row, shift_row):
    center = residual - jnp.mean(residual, axis=-1, keepdims=True)
    spread = jnp.mean(center * center, axis=-1, keepdims=True)
    return center * lax.rsqrt(spread + norm_epsilon) * gain_row + shift_row


def exact_gelu(upper_pre):
    return jax.nn.gelu(upper_pre, approximate=False)


def group_layout(group_lengths, row_count):
    slot_sizes = (group_lengths + SPAN - 1) // SPAN * SPAN
    slot_ends = jnp.cumsum(slot_sizes)
    slot_starts = slot_ends - slot_sizes
    positions = jnp.arange(row_count, dtype=jnp.int32)
    member = (positions[:, None] >= slot_starts[None, :]) & (
        positions[:, None] < slot_ends[None, :]
    )
    seq_first = jnp.sum(jnp.where(member, slot_starts[None, :], 0), axis=1)
    length = jnp.sum(jnp.where(member, group_lengths[None, :], 0), axis=1)
    seq_numbers = jnp.arange(group_lengths.shape[0], dtype=jnp.int32)
    owners = jnp.sum(jnp.where(member, seq_numbers[None, :], 0), axis=1)
    offset = positions - seq_first
    live_rows = (offset < length).astype(jnp.float32)
    angles = 0.5 * math.pi * offset.astype(jnp.float32) / length.astype(jnp.float32)
    cosine = jnp.cos(angles)
    sine_part = jnp.sin(angles)
    span_owner = owners[::SPAN]
    span_order = jnp.arange(span_owner.shape[0], dtype=jnp.int32)
    same_seq = span_owner[None, :] == span_owner[:, None]
    earlier = (same_seq & (span_order[None, :] < span_order[:, None])).astype(jnp.float32)
    return (cosine, sine_part, live_rows, earlier)


def attend(query_rows, key_rows, value_rows, cosine, sine_part, live_rows, earlier):
    row_count = query_rows.shape[0]
    blocks = row_count // SPAN
    soft_query = jax.nn.softplus(query_rows)
    soft_key = jax.nn.softplus(key_rows)
    feat_query = (
        jnp.concatenate([soft_query * cosine[:, None], soft_query * sine_part[:, None]], axis=1)
        * live_rows[:, None]
    )
    feat_key = (
        jnp.concatenate([soft_key * cosine[:, None], soft_key * sine_part[:, None]], axis=1)
        * live_rows[:, None]
    )
    block_query = feat_query.reshape(blocks, SPAN, -1)
    block_key = feat_key.reshape(blocks, SPAN, -1)
    block_value = value_rows.reshape(blocks, SPAN, -1)
    lower_mask = (jnp.arange(SPAN)[:, None] >= jnp.arange(SPAN)[None, :]).astype(jnp.float32)
    scores = jnp.einsum("cik,cjk->cij", block_query, block_key, precision=highest) * lower_mask
    inner_sum = jnp.einsum("cij,cjd->cid", scores, block_value, precision=highest)
    inner_den = jnp.sum(scores, axis=2)
    states = jnp.einsum("cjk,cjd->ckd", block_key, block_value, precision=highest)
    key_sums = jnp.sum(block_key, axis=1)
    before = jnp.einsum("ce,ekd->ckd", earlier, states, precision=highest)
    before_sums = jnp.einsum("ce,ek->ck", earlier, key_sums, precision=highest)
    outer_sum = jnp.einsum("cik,ckd->cid", block_query, before, precision=highest)
    outer_den = jnp.einsum("cik,ck->ci", block_query, before_sums, precision=highest)
    numerator = (inner_sum + outer_sum).reshape(row_count, -1)
    denominator = (inner_den + outer_den).reshape(row_count) + (1.0 - live_rows)
    return numerator / denominator[:, None]


def contract_rows(left, right):
    return lax.dot_general(
        left, right, (((0,), (0,)), ((), ())), preferred_element_type=jnp.float32
    )


def contract_cols(left, right):
    return lax.dot_general(
        left, right, (((1,), (1,)), ((), ())), preferred_element_type=jnp.float32
    )


def adam_update(master, first, second, gradient, rate, decay):
    first_new = first_decay * first + (1.0 - first_decay) * gradient
    second_new = second_decay * second + (1.0 - second_decay) * gradient * gradient
    first_hat = first_new / (1.0 - first_decay**STEP)
    second_hat = second_new / (1.0 - second_decay**STEP)
    master_new = master - rate * (
        first_hat / (jnp.sqrt(second_hat) + adam_epsilon) + decay * master
    )
    return (first_new, second_new, master_new)


def shards(
    tokens,
    cotangent,
    lengths,
    qkv_master,
    out_master,
    up_master,
    down_master,
    vector_master,
    qkv_first,
    qkv_second,
    out_first,
    out_second,
    up_first,
    up_second,
    down_first,
    down_second,
    vector_first,
    vector_second,
):
    mix_weight, out_weight, up_weight, down_weight = (
        lax.all_gather(qkv_master.astype(jnp.bfloat16), "dp", axis=0, tiled=True),
        lax.all_gather(out_master.astype(jnp.bfloat16), "dp", axis=0, tiled=True),
        lax.all_gather(up_master.astype(jnp.bfloat16), "dp", axis=0, tiled=True),
        lax.all_gather(down_master.astype(jnp.bfloat16), "dp", axis=0, tiled=True),
    )
    tok_count = tokens.shape[0]
    width = tokens.shape[1]
    mixed_all = jnp.dot(tokens, mix_weight, preferred_element_type=jnp.float32) + vector_master[
        6:9
    ].reshape(-1)
    mixed_low = mixed_all.astype(jnp.bfloat16)
    query_part = mixed_low[:, :width].reshape(tok_count, H, 1, HD)
    key_part = mixed_low[:, width : 2 * width].reshape(tok_count, H, 1, HD)
    paired = jnp.concatenate([query_part, key_part], axis=2)
    paired = jnp.repeat(paired[:, :, None], 2, axis=2).reshape(tok_count, 4 * width)
    value_part = mixed_low[:, 2 * width :]
    paired_in, values_in = (
        lax.all_to_all(paired, "head", split_axis=1, concat_axis=0, tiled=True),
        lax.all_to_all(value_part, "head", split_axis=1, concat_axis=0, tiled=True),
    )
    group_rows = paired_in.shape[0]
    item_count = paired_in.shape[1] // (2 * HD)
    cosine, sine_part, live_rows, earlier = group_layout(lengths, group_rows)
    stacked = paired_in.reshape(group_rows, item_count, 2, HD).astype(jnp.float32)
    query_items = stacked[:, :, 0]
    key_items = stacked[:, :, 1]
    value_items = values_in.reshape(group_rows, item_count, HD // 2).astype(jnp.float32)

    def mix_items(query_set, key_set, value_set):

        def single(query_rows, key_rows, value_rows):
            return attend(query_rows, key_rows, value_rows, cosine, sine_part, live_rows, earlier)

        return jax.vmap(single, in_axes=1, out_axes=1)(query_set, key_set, value_set)

    attended, mix_back = jax.vjp(mix_items, query_items, key_items, value_items)
    heads_out = attended.reshape(group_rows, item_count * (HD // 2)).astype(jnp.bfloat16)
    heads = lax.all_to_all(heads_out, "head", split_axis=0, concat_axis=1, tiled=True)
    projected = jnp.dot(heads, out_weight, preferred_element_type=jnp.float32) + vector_master[4]
    resid_one = tokens.astype(jnp.float32) + projected
    hidden, norm_one_back = jax.vjp(layer_norm, resid_one, vector_master[0], vector_master[1])
    hidden_low = hidden.astype(jnp.bfloat16)
    upper_pre = jnp.dot(hidden_low, up_weight, preferred_element_type=jnp.float32) + vector_master[
        9:13
    ].reshape(-1)
    active, gelu_back = jax.vjp(exact_gelu, upper_pre)
    active_low = active.astype(jnp.bfloat16)
    lowered = (
        jnp.dot(active_low, down_weight, preferred_element_type=jnp.float32) + vector_master[5]
    )
    output, norm_two_back = jax.vjp(
        layer_norm, hidden + lowered, vector_master[2], vector_master[3]
    )
    grad_two, gain_two, shift_two = norm_two_back(cotangent)
    grad_two_low = grad_two.astype(jnp.bfloat16)
    down_grad = contract_rows(active_low, grad_two_low)
    (upper_grad,) = gelu_back(contract_cols(grad_two_low, down_weight))
    upper_low = upper_grad.astype(jnp.bfloat16)
    up_grad = contract_rows(hidden_low, upper_low)
    hidden_grad = grad_two + contract_cols(upper_low, up_weight)
    grad_one, gain_one, shift_one = norm_one_back(hidden_grad)
    grad_one_low = grad_one.astype(jnp.bfloat16)
    out_grad = contract_rows(heads, grad_one_low)
    heads_grad = contract_cols(grad_one_low, out_weight).astype(jnp.bfloat16)
    heads_back = lax.all_to_all(heads_grad, "head", split_axis=1, concat_axis=0, tiled=True)
    query_back, key_back, value_back = mix_back(
        heads_back.reshape(group_rows, item_count, HD // 2).astype(jnp.float32)
    )
    pair_back = (
        jnp.stack([query_back, key_back], axis=2)
        .astype(jnp.bfloat16)
        .reshape(group_rows, item_count * 2 * HD)
    )
    value_low = value_back.astype(jnp.bfloat16).reshape(group_rows, item_count * (HD // 2))
    pair_home, value_home = (
        lax.all_to_all(pair_back, "head", split_axis=0, concat_axis=1, tiled=True),
        lax.all_to_all(value_low, "head", split_axis=0, concat_axis=1, tiled=True),
    )
    summed = jnp.sum(pair_home.astype(jnp.float32).reshape(tok_count, H, 2, 2, HD), axis=2)
    mixed_grad = jnp.concatenate(
        [
            summed[:, :, 0].reshape(tok_count, width),
            summed[:, :, 1].reshape(tok_count, width),
            value_home.astype(jnp.float32),
        ],
        axis=1,
    )
    mixed_low_grad = mixed_grad.astype(jnp.bfloat16)
    mix_grad = contract_rows(tokens, mixed_low_grad)
    input_grad = grad_one + contract_cols(mixed_low_grad, mix_weight)
    vector_grad = jnp.concatenate(
        [
            jnp.stack(
                [
                    gain_one,
                    shift_one,
                    gain_two,
                    shift_two,
                    jnp.sum(grad_one, axis=0),
                    jnp.sum(grad_two, axis=0),
                ]
            ),
            jnp.sum(mixed_grad, axis=0).reshape(3, width),
            jnp.sum(upper_grad, axis=0).reshape(4, width),
        ],
        axis=0,
    )
    local_grads = (mix_grad, out_grad, up_grad, down_grad)
    row_parts = (
        lax.psum_scatter(
            local_grads[0].astype(jnp.bfloat16), "dp", scatter_dimension=0, tiled=True
        ).astype(jnp.float32),
        lax.psum_scatter(
            local_grads[1].astype(jnp.bfloat16), "dp", scatter_dimension=0, tiled=True
        ).astype(jnp.float32),
        lax.psum_scatter(
            local_grads[2].astype(jnp.bfloat16), "dp", scatter_dimension=0, tiled=True
        ).astype(jnp.float32),
        lax.psum_scatter(
            local_grads[3].astype(jnp.bfloat16), "dp", scatter_dimension=0, tiled=True
        ).astype(jnp.float32),
    )
    reduced = (
        lax.psum(row_parts[0].astype(jnp.bfloat16), "head").astype(jnp.float32),
        lax.psum(row_parts[1].astype(jnp.bfloat16), "head").astype(jnp.float32),
        lax.psum(row_parts[2].astype(jnp.bfloat16), "head").astype(jnp.float32),
        lax.psum(row_parts[3].astype(jnp.bfloat16), "head").astype(jnp.float32),
    )
    vector_total = lax.psum(vector_grad, ("dp", "head"))
    qkv_new = adam_update(
        qkv_master, qkv_first, qkv_second, reduced[0], 1.0 / math.sqrt(D), weight_decay
    )
    out_new = adam_update(
        out_master, out_first, out_second, reduced[1], 1.0 / math.sqrt(OUT_FAN), weight_decay
    )
    up_new = adam_update(
        up_master, up_first, up_second, reduced[2], 1.0 / math.sqrt(D), weight_decay
    )
    down_new = adam_update(
        down_master, down_first, down_second, reduced[3], 1.0 / math.sqrt(FF), weight_decay
    )
    vector_new = adam_update(
        vector_master, vector_first, vector_second, vector_total, vector_rate, 0.0
    )
    return (
        output.astype(jnp.bfloat16),
        input_grad,
        qkv_new[0],
        qkv_new[1],
        qkv_new[2],
        out_new[0],
        out_new[1],
        out_new[2],
        up_new[0],
        up_new[1],
        up_new[2],
        down_new[0],
        down_new[1],
        down_new[2],
        vector_new[0],
        vector_new[1],
        vector_new[2],
    )


def solution(mesh):
    return jax.shard_map(
        shards,
        mesh=mesh,
        in_specs=(
            P(("dp", "head"), None),
            P(("dp", "head"), None),
            P("dp"),
            P("dp", None),
            P("dp", None),
            P("dp", None),
            P("dp", None),
            P(),
            P("dp", None),
            P("dp", None),
            P("dp", None),
            P("dp", None),
            P("dp", None),
            P("dp", None),
            P("dp", None),
            P("dp", None),
            P(),
            P(),
        ),
        out_specs=(
            P(("dp", "head"), None),
            P(("dp", "head"), None),
            P("dp", None),
            P("dp", None),
            P("dp", None),
            P("dp", None),
            P("dp", None),
            P("dp", None),
            P("dp", None),
            P("dp", None),
            P("dp", None),
            P("dp", None),
            P("dp", None),
            P("dp", None),
            P(),
            P(),
            P(),
        ),
        check_vma=False,
    )
```

profile of v0, /device:TPU:0, one launch (start us, length us, event | category | flops | bytes accessed | tf_op | source)
XLA Modules:
  0.0 781.5 jit_solution(3843467809521252633)
XLA Ops:
  12.1 35.1 %all-gather.5.cloned.1.call-done = bf16[768,2304]{1,0:T(8,128)(2,1)} async-done(((bf16[96,2304]{1,0:T(8,128)(2,1)}), bf16[768,2304]{1,0:T(8,128)(2,1)}) %all-gather.5.cloned.1.call-update) | async-done | bytes 3538960 | tf_op jit(solution)/shard_map/all_gather | solution.py:135
  47.2 4.0 fusion.16
  52.5 4.6 all-to-all-start.1
  58.0 19.7 %all-to-all-done.1 = bf16[512,4,192]{0,2,1:T(8,128)(2,1)S(1)} async-done(((bf16[512,4,192]{0,2,1:T(8,128)(2,1)}), bf16[512,4,192]{0,2,1:T(8,128)(2,1)S(1)}, u32[]{:S(2)}, u32[]{:S(2)}) %all-to-all-start.1) | async-done | bytes 786464 | tf_op jit(solution)/shard_map/all_to_all | solution.py:153
  79.8 4.8 all-to-all-start
  90.2 64.7 %all-to-all-done = bf16[512,4,768]{0,2,1:T(8,128)(2,1)} async-done(((bf16[512,4,768]{0,2,1:T(8,128)(2,1)}), bf16[512,4,768]{0,2,1:T(8,128)(2,1)}, u32[]{:S(2)}, u32[]{:S(2)}) %all-to-all-start) | async-done | bytes 3145760 | tf_op jit(solution)/shard_map/all_to_all | solution.py:152
  154.9 2.8 convert_bitcast_fusion
  157.7 6.7 copy.198
  164.4 8.5 %reshape.335 = f32[2048,6,2,64]{0,3,2,1:T(8,128)} reshape(f32[4,512,768]{1,0,2:T(4,128)} %copy.198) | data formatting | bytes 12582912 | tf_op jit(solution)/shard_map/convert_element_type | solution.py:158
  172.8 8.2 %multiply_bitcast_fusion.1 = (f32[6,2048,64]{1,2,0:T(8,128)}, f32[6,2048,64]{1,2,0:T(8,128)}, f32[6,2048,64]{1,2,0:T(8,128)}, f32[6,2048,64]{1,2,0:T(8,128)}) fusion(f32[2048]{0:T(1024)S(1)} %get-tuple-element.156, f32[2048,6,2,64]{0,3,2,1:T(8,128)} %reshape.335, f32[2048]{0:T(1024)S(1)} %get-tuple-element.155), kind=kLoop, calls=%fused_computation.83 | loop fusion | flops 12582912 | bytes 18890752 | tf_op jit(solution)/shard_map/jvp(vmap())/mul | solution.py:70
  181.0 5.8 copy.251
  186.8 5.8 copy.249
  192.6 5.8 copy.250
  198.4 5.7 copy.252
  204.1 10.3 %fusion.131 = (f32[6,32,128]{2,1,0:T(8,128)S(1)}, f32[6,32,64,128]{3,2,1,0:T(8,128)S(1)}, f32[6,32,64,128]{3,2,1,0:T(8,128)S(1)}) fusion(f32[32,64]{1,0:T(8,128)S(1)} %fusion.97, f32[6,32,64,64]{3,2,1,0:T(8,128)} %bitcast.197, f32[6,32,64,64]{3,2,1,0:T(8,128)} %bitcast.194, f32[6,32,64,64]{3,2,1,0:T(8,128)} %bitcast.196, f32[6,32,64,64]{3,2,1,0:T(8,128)} %bitcast.195), kind=kLoop, calls=%fused_computation.216 | loop fusion | flops 7839744 | bytes 25272320 | tf_op jit(solution)/shard_map/jvp(vmap())/reduce_sum | solution.py:81
  214.8 3.6 fusion.84
  218.5 5.3 fusion.35
  223.8 10.0 %fusion.137 = f32[6,32,1,64]{3,2,1,0:T(1,128)S(1)} fusion(f32[6,32,64,128]{3,2,1,0:T(8,128)S(1)} %get-tuple-element.157, f32[32,6,128,1]{2,3,0,1:T(1,128)S(1)} %bitcast.216), kind=kOutput, calls=%fused_computation.222 | convolution fusion | flops 18874368 | bytes 6438912 | tf_op jit(solution)/shard_map/jvp(vmap(cik,ck->ci))/dot_general | solution.py:85
  233.8 12.0 %multiply_reduce_fusion = (f32[6,32,64]{2,1,0:T(8,128)S(1)}, f32[6,32,64,64]{2,3,1,0:T(8,128)}) fusion(f32[64,64]{0,1:T(8,128)S(1)} %fusion.96, f32[6,32,64,128]{3,2,1,0:T(8,128)S(1)} %get-tuple-element.157, f32[6,32,64,128]{3,2,1,0:T(8,128)S(1)} %get-tuple-element.138), kind=kOutput, calls=%fused_computation.37 | convolution fusion | flops 1209520128 | bytes 15794176 | tf_op jit(solution)/shard_map/jvp(vmap(cik,cjk->cij))/dot_general | solution.py:77
  246.0 14.2 %fusion.49 = f32[6,32,64,32]{2,3,1,0:T(8,128)S(1)} fusion(f32[6,32,64,128]{3,2,1,0:T(8,128)} %copy-done, f32[32,6,128,32]{2,0,3,1:T(8,128)} %fusion.35), kind=kOutput, calls=%fused_computation.92 | convolution fusion | flops 603979776 | bytes 11010048 | tf_op jit(solution)/shard_map/jvp(vmap(cik,ckd->cid))/dot_general | solution.py:84
  260.2 3.5 fusion.62
  263.7 3.5 copy.212
  267.2 2.9 reshape.324
  271.9 3.5 all-to-all-start.2
  275.6 19.3 %all-to-all-done.2 = bf16[4,512,192]{1,2,0:T(8,128)(2,1)S(1)} async-done(((bf16[4,512,192]{1,2,0:T(8,128)(2,1)}), bf16[4,512,192]{1,2,0:T(8,128)(2,1)S(1)}, u32[]{:S(2)}, u32[]{:S(2)}) %all-to-all-start.2) | async-done | bytes 786464 | tf_op jit(solution)/shard_map/all_to_all | solution.py:172
  295.8 2.6 fusion.134
  298.8 19.9 %multiply_convert_fusion = (bf16[512,3072]{1,0:T(8,128)(2,1)}, f32[512,3072]{1,0:T(8,128)}, f32[512,3072]{1,0:T(8,128)}) fusion(f32[3072]{0:T(1024)S(1)} %add.230, bf16[768,3072]{1,0:T(8,128)(2,1)} %all-gather.9.cloned.1.call-done, f32[512,768]{1,0:T(8,128)S(1)} %get-tuple-element.163, f32[768]{0:T(1024)S(1)} %get-tuple-element.101, ...), kind=kOutput, calls=%fused_computation.15 | convolution fusion | flops 2521694208 | bytes 22042624 | tf_op jit(solution)/shard_map/dot_general | solution.py:177
  318.6 6.1 fusion.135
  328.6 9.9 %fusion.136 = (f32[3072]{0:T(1024)}, bf16[512,3072]{1,0:T(8,128)(2,1)}) fusion(f32[512,3072]{1,0:T(8,128)} %get-tuple-element.134, bf16[3072,768]{1,0:T(8,128)(2,1)S(1)} %copy-done.47, f32[512,768]{1,0:T(8,128)S(1)} %get-tuple-element.132, f32[512]{0:T(512)S(1)} %negate_multiply_fusion.2, f32[512,3072]{1,0:T(8,128)} %get-tuple-element.164, f32[3072]{0:T(1024)S(1)} %add.230), kind=kOutput, calls=%fused_computation.221 | convolution fusion | flops 2441868288 | bytes 22046720 | tf_op jit(solution)/shard_map/dot_general | solution.py:98
  338.5 5.6 multiply_reduce_fusion.2
  348.0 7.4 convolution_convert_fusion.1
  355.4 3.5 convolution_convert_fusion.4
  361.2 4.2 all-to-all-start.3
  365.9 7.0 convolution_convert_fusion
  372.9 12.2 %all-to-all-done.3 = bf16[512,4,192]{0,2,1:T(8,128)(2,1)} async-done(((bf16[512,4,192]{0,2,1:T(8,128)(2,1)}), bf16[512,4,192]{0,2,1:T(8,128)(2,1)}, u32[]{:S(2)}, u32[]{:S(2)}) %all-to-all-start.3) | async-done | bytes 786464 | tf_op jit(solution)/shard_map/all_to_all | solution.py:199
  389.6 2.9 fusion.68
  392.7 3.8 reshape.326
  396.5 14.7 %fusion.12 = f32[6,32,64,32]{2,3,1,0:T(8,128)S(1)} fusion(f32[6,32,64,64]{2,3,1,0:T(8,128)} %get-tuple-element.161, f32[64,64]{0,1:T(8,128)S(1)} %fusion.96, f32[6,32,64,32]{2,1,3,0:T(8,128)} %reshape.326), kind=kOutput, calls=%fused_computation.35 | convolution fusion | flops 302776320 | bytes 6307840 | tf_op jit(solution)/shard_map/transpose(jvp(vmap(cij,cjd->cid)))/dot_general | solution.py:78
  411.3 8.0 %fusion.8 = f32[32,6,128,32]{2,3,1,0:T(8,128)S(1)} fusion(f32[6,32,64,128]{3,2,1,0:T(8,128)S(1)} %bitcast.187, f32[6,32,64,32]{2,1,3,0:T(8,128)S(1)} %copy-done.2), kind=kOutput, calls=%fused_computation.31 | convolution fusion | flops 603979776 | bytes 11010048 | tf_op jit(solution)/shard_map/transpose(jvp(vmap(cik,ckd->cid)))/dot_general | solution.py:84
  419.3 6.2 fusion.52
  425.5 5.5 fusion.6
  431.2 3.7 fusion.59
  434.9 6.4 fusion.45
  441.3 11.1 %add_convert_fusion = bf16[6,32,64,32]{2,3,1,0:T(8,128)(2,1)S(1)} fusion(f32[6,32,64,32]{2,3,1,0:T(8,128)S(1)} %fusion.12, f32[6,32,64,128]{3,2,1,0:T(8,128)S(1)} %bitcast.189, f32[6,32,128,32]{2,1,3,0:T(8,128)S(1)} %fusion.59), kind=kOutput, calls=%fused_computation.73 | convolution fusion | flops 604766208 | bytes 11796480 | tf_op jit(solution)/shard_map/transpose(jvp(vmap(cjk,cjd->ckd)))/dot_general | solution.py:80
  456.1 4.2 all-to-all-start.5
  460.3 13.0 %fusion.11 = f32[6,32,64,128]{3,2,1,0:T(8,128)S(1)} fusion(f32[6,32,64,128]{3,2,1,0:T(8,128)} %copy-done.1, f32[6,32,64,64]{2,3,1,0:T(8,128)} %fusion.52, f32[6,32,64]{2,1,0:T(8,128)S(1)} %neg.30, f32[64,64]{0,1:T(8,128)S(1)} %fusion.96), kind=kOutput, calls=%fused_computation.34 | convolution fusion | flops 1209532416 | bytes 15794176 | tf_op jit(solution)/shard_map/transpose(jvp(vmap(cik,cjk->cij)))/dot_general | solution.py:77
  473.3 15.4 %add_add_fusion.1 = f32[6,32,64,128]{3,2,1,0:T(8,128)} fusion(f32[6,32,64,128]{3,2,1,0:T(8,128)S(1)} %fusion.11, f32[6,32,128]{2,1,0:T(8,128)S(1)} %bitcast.217, f32[6,32,64]{2,1,0:T(8,128)S(1)} %neg.30, f32[32,6,128,32]{2,0,3,1:T(8,128)S(1)} %copy-done.7, f32[6,32,64,32]{2,1,3,0:T(8,128)S(1)} %copy-done.3), kind=kOutput, calls=%fused_computation.13 | convolution fusion | flops 608698368 | bytes 17448960 | tf_op jit(solution)/shard_map/transpose(jvp(vmap(cik,ckd->cid)))/dot_general | solution.py:84
  488.7 6.6 copy.223
  495.3 13.2 %add_add_fusion = f32[6,32,64,128]{3,2,1,0:T(8,128)} fusion(f32[6,32,64,128]{3,2,1,0:T(8,128)} %fusion.45, f32[6,32,128]{2,1,0:T(8,128)S(1)} %convolution_bitcast_fusion, f32[6,32,64,128]{3,2,1,0:T(8,128)} %copy-done, f32[6,32,64,64]{2,3,1,0:T(8,128)} %fusion.52, f32[6,32,64]{2,1,0:T(8,128)S(1)} %neg.30, f32[64,64]{0,1:T(8,128)S(1)} %fusion.96), kind=kOutput, calls=%fused_computation.11 | convolution fusion | flops 1212678144 | bytes 22183936 | tf_op jit(solution)/shard_map/transpose(jvp(vmap(cik,cjk->cij)))/dot_general | solution.py:77
  508.6 6.7 copy.229
  515.3 12.0 %broadcast_multiply_fusion.1 = (f32[6,2048,128]{1,2,0:T(8,128)}, f32[6,2048,128]{1,2,0:T(8,128)}) fusion(f32[6,2048,128]{1,2,0:T(8,128)} %copy.223, f32[2048]{0:T(1024)S(1)} %copy-done.42, f32[6,2048,128]{1,2,0:T(8,128)} %copy.229), kind=kLoop, calls=%fused_computation.75 | loop fusion | flops 3145728 | bytes 25174016 | tf_op jit(solution)/shard_map/transpose(jvp(vmap()))/mul | solution.py:66
  527.3 8.5 %fusion.73 = (bf16[2048,6,1,64]{0,3,1,2:T(8,128)(2,1)S(1)}, bf16[2048,6,1,64]{0,3,1,2:T(8,128)(2,1)S(1)}) fusion(f32[2048,6,2,64]{0,3,2,1:T(8,128)S(1)} %bitcast.193, f32[2048]{0:T(1024)S(1)} %copy-done.39, f32[6,2048,128]{1,2,0:T(8,128)} %get-tuple-element.158, f32[2048]{0:T(1024)S(1)} %copy-done.37, f32[6,2048,128]{1,2,0:T(8,128)} %get-tuple-element.159), kind=kLoop, calls=%fused_computation.125 | loop fusion | flops 25165824 | bytes 22036480 | tf_op jit(solution)/shard_map/stack | solution.py:204
  536.4 4.0 convert_element_type.208
  540.4 4.1 copy.231
  544.5 5.0 all-to-all-start.4
  552.3 67.2 %all-to-all-done.4 = bf16[4,512,768]{1,2,0:T(8,128)(2,1)S(1)} async-done(((bf16[4,512,768]{1,2,0:T(8,128)(2,1)}), bf16[4,512,768]{1,2,0:T(8,128)(2,1)S(1)}, u32[]{:S(2)}, u32[]{:S(2)}) %all-to-all-start.4) | async-done | bytes 3145760 | tf_op jit(solution)/shard_map/all_to_all | solution.py:210
  619.5 3.5 convert_element_type.232
  623.1 3.9 reduce_sum.263
  631.4 4.0 copy.255
  635.6 46.4 %reduce-scatter.13.cloned.1.call-done = bf16[96,2304]{1,0:T(8,128)(2,1)} async-done(((bf16[768,2304]{1,0:T(8,128)(2,1)}), bf16[96,2304]{1,0:T(8,128)(2,1)}) %reduce-scatter.13.cloned.1.call-update) | async-done | bytes 442384 | tf_op jit(solution)/shard_map/reduce_scatter | solution.py:244
  686.0 43.5 %psum.39 = f32[13,768]{1,0:T(8,128)S(1)} all-reduce(f32[13,768]{1,0:T(8,128)S(1)} %concatenate.33), channel_id=1, replica_groups=mesh['dp'=8,'head'=4] {'dp','head'}, use_global_device_ids=true, to_apply=%region_32.34 | all-reduce | flops 9984 | bytes 79872 | tf_op jit(solution)/shard_map/psum | solution.py:263
  730.2 6.4 convolution_add_fusion.1
  736.6 26.0 %all-reduce.3.cloned.1.call-done = (bf16[96,2304]{1,0:T(8,128)(2,1)}, bf16[96,768]{1,0:T(8,128)(2,1)}, bf16[96,3072]{1,0:T(8,128)(2,1)}, bf16[384,768]{1,0:T(8,128)(2,1)}) async-done(((bf16[96,2304]{1,0:T(8,128)(2,1)}, bf16[96,768]{1,0:T(8,128)(2,1)}, bf16[96,3072]{1,0:T(8,128)(2,1)}, bf16[384,768]{1,0:T(8,128)(2,1)}), (bf16[96,2304]{1,0:T(8,128)(2,1)}, bf16[96,768]{1,0:T(8,128)(2,1)}, ...) | async-done | bytes 1769488 | tf_op jit(solution)/shard_map/psum | solution.py:258
  764.8 3.9 multiply_subtract_fusion.2
  (233 shorter events, 57.3 us)
Async XLA Ops:
  7.2 4.0 copy-start.21
  7.2 4.9 copy-start.34
  7.2 40.0 %copy-start.48 = (bf16[512,768]{1,0:T(8,128)(2,1)S(1)}, bf16[512,768]{1,0:T(8,128)(2,1)}, u32[]{:S(2)}) copy-start(bf16[512,768]{1,0:T(8,128)(2,1)} %param.19) | copy-start | bytes 2359300
  7.2 40.0 %all-gather.5.cloned.1.call-start = ((), (), s32[]{:S(2)}) async-start(), calls=%async_computation.10 | async-start | bytes 3981312 | tf_op jit(solution)/shard_map/all_gather | solution.py:135
  9.4 266.2 %all-gather.7.cloned.1.call-start = ((), (), s32[]{:S(2)}) async-start(), calls=%async_computation.11 | async-start | bytes 1327104 | tf_op jit(solution)/shard_map/all_gather | solution.py:136
  11.1 287.7 %all-gather.9.cloned.1.call-start = ((), (), s32[]{:S(2)}) async-start(), calls=%async_computation.12 | async-start | bytes 5308416 | tf_op jit(solution)/shard_map/all_gather | solution.py:137
  52.5 25.1 %all-to-all-start.1 = ((bf16[512,4,192]{0,2,1:T(8,128)(2,1)}), bf16[512,4,192]{0,2,1:T(8,128)(2,1)S(1)}, u32[]{:S(2)}, u32[]{:S(2)}) async-start(bf16[512,4,192]{0,2,1:T(8,128)(2,1)} %bitcast.16), calls=%async_computation.1 | async-start | bytes 1572864 | tf_op jit(solution)/shard_map/all_to_all | solution.py:153
  79.8 4.9 copy-start.23
  79.8 5.8 copy-start.46
  79.8 75.1 %all-to-all-start = ((bf16[512,4,768]{0,2,1:T(8,128)(2,1)}), bf16[512,4,768]{0,2,1:T(8,128)(2,1)}, u32[]{:S(2)}, u32[]{:S(2)}) async-start(bf16[512,4,768]{0,2,1:T(8,128)(2,1)} %bitcast.2), calls=%async_computation | async-start | bytes 6291456 | tf_op jit(solution)/shard_map/all_to_all | solution.py:152
  84.6 234.0 %all-gather.11.cloned.1.call-start = ((), (), s32[]{:S(2)}) async-start(), calls=%async_computation.13 | async-start | bytes 5308416 | tf_op jit(solution)/shard_map/all_gather | solution.py:138
  86.8 86.0 %copy-start.36 = (f32[2048]{0:T(1024)}, f32[2048]{0:T(1024)S(1)}, u32[]{:S(2)}) copy-start(f32[2048]{0:T(1024)S(1)} %get-tuple-element.155) | copy-start | bytes 24580
  86.8 86.0 %copy-start.38 = (f32[2048]{0:T(1024)}, f32[2048]{0:T(1024)S(1)}, u32[]{:S(2)}) copy-start(f32[2048]{0:T(1024)S(1)} %get-tuple-element.156) | copy-start | bytes 24580
  90.1 124.7 %copy-start.4 = (bf16[6,32,64,32]{2,1,3,0:T(8,128)(2,1)}, bf16[6,32,64,32]{2,1,3,0:T(8,128)(2,1)S(1)}, u32[]{:S(2)}) copy-start(bf16[6,32,64,32]{2,1,3,0:T(8,128)(2,1)S(1)} %reshape.323) | copy-start | bytes 2359300
  214.5 19.3 %copy-start = (f32[6,32,64,128]{3,2,1,0:T(8,128)}, f32[6,32,64,128]{3,2,1,0:T(8,128)S(1)}, u32[]{:S(2)}) copy-start(f32[6,32,64,128]{3,2,1,0:T(8,128)S(1)} %get-tuple-element.157) | copy-start | bytes 18874372
  214.5 19.3 %copy-start.1 = (f32[6,32,64,128]{3,2,1,0:T(8,128)}, f32[6,32,64,128]{3,2,1,0:T(8,128)S(1)}, u32[]{:S(2)}) copy-start(f32[6,32,64,128]{3,2,1,0:T(8,128)S(1)} %get-tuple-element.138) | copy-start | bytes 18874372
  245.8 14.3 %slice-start.4 = ((s8[6291456]{0:T(1024)(128)(4,1)}), s8[2097152]{0:T(1024)(128)(4,1)S(1)}, s32[]{:S(2)}) async-start(s8[6291456]{0:T(1024)(128)(4,1)} %bitcast.190), calls=%async_computation.23 | async-start | bytes 4194304
  245.9 14.2 %slice-start.5 = ((s8[6291456]{0:T(1024)(128)(4,1)}), s8[4194304]{0:T(1024)(128)(4,1)S(1)}, s32[]{:S(2)}) async-start(s8[6291456]{0:T(1024)(128)(4,1)} %bitcast.190), calls=%async_computation.24 | async-start | bytes 8388608
  245.9 14.2 %copy-start.5 = (bf16[6,32,64,32]{2,1,3,0:T(8,128)(2,1)S(1)}, bf16[6,32,64,32]{2,1,3,0:T(8,128)(2,1)}, u32[]{:S(2)}) copy-start(bf16[6,32,64,32]{2,1,3,0:T(8,128)(2,1)} %copy-done.4) | copy-start | bytes 2359300
  271.9 23.0 %all-to-all-start.2 = ((bf16[4,512,192]{1,2,0:T(8,128)(2,1)}), bf16[4,512,192]{1,2,0:T(8,128)(2,1)S(1)}, u32[]{:S(2)}, u32[]{:S(2)}) async-start(bf16[4,512,192]{1,2,0:T(8,128)(2,1)} %copy.214), calls=%async_computation.2 | async-start | bytes 1572864 | tf_op jit(solution)/shard_map/all_to_all | solution.py:172
  275.4 360.2 %reduce-scatter.7.cloned.1.call-start = ((), (), s32[]{:S(2)}) async-start(), calls=%async_computation.14 | async-start | bytes 1327104 | tf_op jit(solution)/shard_map/reduce_scatter | solution.py:247
  298.4 20.2 %copy-start.15 = (f32[512,768]{1,0:T(8,128)}, f32[512,768]{1,0:T(8,128)S(1)}, u32[]{:S(2)}) copy-start(f32[512,768]{1,0:T(8,128)S(1)} %get-tuple-element.163) | copy-start | bytes 4718596
  318.6 6.5 copy-start.17
  325.8 2.8 copy-start.47
  325.8 12.7 %slice-start.8 = ((s8[4718592]{0:T(1024)(128)(4,1)}), s8[4194304]{0:T(1024)(128)(4,1)S(1)}, s32[]{:S(2)}) async-start(s8[4718592]{0:T(1024)(128)(4,1)} %bitcast.222), calls=%async_computation.27 | async-start | bytes 8388608
  327.4 38.5 %copy-start.8 = (f32[512,768]{1,0:T(8,128)}, f32[512,768]{1,0:T(8,128)S(1)}, u32[]{:S(2)}) copy-start(f32[512,768]{1,0:T(8,128)S(1)} %get-tuple-element.132) | copy-start | bytes 4718596
  328.6 9.9 %copy-start.16 = (f32[512,768]{1,0:T(8,128)S(1)}, f32[512,768]{1,0:T(8,128)}, u32[]{:S(2)}) copy-start(f32[512,768]{1,0:T(8,128)} %copy-done.15) | copy-start | bytes 4718596
  328.6 9.9 %slice-start.9 = ((s8[4718592]{0:T(1024)(128)(4,1)}), s8[524288]{0:T(1024)(128)(4,1)S(1)}, s32[]{:S(2)}) async-start(s8[4718592]{0:T(1024)(128)(4,1)} %bitcast.222), calls=%async_computation.28 | async-start | bytes 1048576
  347.9 287.7 %reduce-scatter.9.cloned.1.call-start = ((), (), s32[]{:S(2)}) async-start(), calls=%async_computation.15 | async-start | bytes 5308416 | tf_op jit(solution)/shard_map/reduce_scatter | solution.py:250
  361.2 23.9 %all-to-all-start.3 = ((bf16[512,4,192]{0,2,1:T(8,128)(2,1)}), bf16[512,4,192]{0,2,1:T(8,128)(2,1)}, u32[]{:S(2)}, u32[]{:S(2)}) async-start(bf16[512,4,192]{0,2,1:T(8,128)(2,1)} %bitcast.211), calls=%async_computation.3 | async-start | bytes 1572864 | tf_op jit(solution)/shard_map/all_to_all | solution.py:199
  365.4 270.2 %reduce-scatter.11.cloned.1.call-start = ((), (), s32[]{:S(2)}) async-start(), calls=%async_computation.16 | async-start | bytes 5308416 | tf_op jit(solution)/shard_map/reduce_scatter | solution.py:253
  392.7 18.5 %slice-start = ((s8[6291456]{0:T(1024)(128)(4,1)}), s8[2097152]{0:T(1024)(128)(4,1)S(1)}, s32[]{:S(2)}) async-start(s8[6291456]{0:T(1024)(128)(4,1)} %bitcast.186), calls=%async_computation.19 | async-start | bytes 4194304
  396.5 14.7 %slice-start.1 = ((s8[6291456]{0:T(1024)(128)(4,1)}), s8[4194304]{0:T(1024)(128)(4,1)S(1)}, s32[]{:S(2)}) async-start(s8[6291456]{0:T(1024)(128)(4,1)} %bitcast.186), calls=%async_computation.20 | async-start | bytes 8388608
  396.5 14.7 %copy-start.2 = (f32[6,32,64,32]{2,1,3,0:T(8,128)S(1)}, f32[6,32,64,32]{2,1,3,0:T(8,128)}, u32[]{:S(2)}) copy-start(f32[6,32,64,32]{2,1,3,0:T(8,128)} %reshape.326) | copy-start | bytes 4718596
  411.2 8.0 %copy-start.6 = (bf16[6,32,64,32]{2,1,3,0:T(8,128)(2,1)S(1)}, bf16[6,32,64,32]{2,1,3,0:T(8,128)(2,1)}, u32[]{:S(2)}) copy-start(bf16[6,32,64,32]{2,1,3,0:T(8,128)(2,1)} %copy-done.4) | copy-start | bytes 2359300
  431.2 10.1 %slice-start.2 = ((s8[6291456]{0:T(1024)(128)(4,1)}), s8[4194304]{0:T(1024)(128)(4,1)S(1)}, s32[]{:S(2)}) async-start(s8[6291456]{0:T(1024)(128)(4,1)} %bitcast.188), calls=%async_computation.21 | async-start | bytes 8388608
  434.9 6.4 slice-start.3
  456.1 88.4 %all-to-all-start.5 = ((bf16[4,512,192]{1,2,0:T(8,128)(2,1)}), bf16[4,512,192]{1,2,0:T(8,128)(2,1)}, u32[]{:S(2)}, u32[]{:S(2)}) async-start(bf16[4,512,192]{1,2,0:T(8,128)(2,1)} %copy.236), calls=%async_computation.5 | async-start | bytes 1572864 | tf_op jit(solution)/shard_map/all_to_all | solution.py:211
  460.3 13.0 %copy-start.3 = (f32[6,32,64,32]{2,1,3,0:T(8,128)S(1)}, f32[6,32,64,32]{2,1,3,0:T(8,128)}, u32[]{:S(2)}) copy-start(f32[6,32,64,32]{2,1,3,0:T(8,128)} %reshape.326) | copy-start | bytes 4718596
  460.3 13.0 %copy-start.7 = (f32[32,6,128,32]{2,0,3,1:T(8,128)S(1)}, f32[32,6,128,32]{2,0,3,1:T(8,128)}, u32[]{:S(2)}) copy-start(f32[32,6,128,32]{2,0,3,1:T(8,128)} %fusion.35) | copy-start | bytes 9437188
  508.6 6.7 copy-start.42
  515.3 12.0 %slice-start.6 = ((s8[6291456]{0:T(1024)(128)(4,1)}), s8[4194304]{0:T(1024)(128)(4,1)S(1)}, s32[]{:S(2)}) async-start(s8[6291456]{0:T(1024)(128)(4,1)} %bitcast.192), calls=%async_computation.25 | async-start | bytes 8388608
  515.3 12.0 %slice-start.7 = ((s8[6291456]{0:T(1024)(128)(4,1)}), s8[2097152]{0:T(1024)(128)(4,1)S(1)}, s32[]{:S(2)}) async-start(s8[6291456]{0:T(1024)(128)(4,1)} %bitcast.192), calls=%async_computation.26 | async-start | bytes 4194304
  515.3 12.0 %copy-start.37 = (f32[2048]{0:T(1024)S(1)}, f32[2048]{0:T(1024)}, u32[]{:S(2)}) copy-start(f32[2048]{0:T(1024)} %copy-done.36) | copy-start | bytes 24580
  515.3 12.0 %copy-start.39 = (f32[2048]{0:T(1024)S(1)}, f32[2048]{0:T(1024)}, u32[]{:S(2)}) copy-start(f32[2048]{0:T(1024)} %copy-done.38) | copy-start | bytes 24580
  544.5 75.0 %all-to-all-start.4 = ((bf16[4,512,768]{1,2,0:T(8,128)(2,1)}), bf16[4,512,768]{1,2,0:T(8,128)(2,1)S(1)}, u32[]{:S(2)}, u32[]{:S(2)}) async-start(bf16[4,512,768]{1,2,0:T(8,128)(2,1)} %copy.231), calls=%async_computation.4 | async-start | bytes 6291456 | tf_op jit(solution)/shard_map/all_to_all | solution.py:210
  549.6 132.5 %reduce-scatter.13.cloned.1.call-start = ((), (), s32[]{:S(2)}) async-start(), calls=%async_computation.17 | async-start | bytes 3981312 | tf_op jit(solution)/shard_map/reduce_scatter | solution.py:244
  635.4 46.7 %copy-start.43 = (f32[3072]{0:T(1024)S(1)}, f32[3072]{0:T(1024)}, u32[]{:S(2)}) copy-start(f32[3072]{0:T(1024)} %get-tuple-element.168) | copy-start | bytes 36868
  635.4 46.7 %copy-start.45 = (f32[768]{0:T(1024)S(1)}, f32[768]{0:T(1024)}, u32[]{:S(2)}) copy-start(f32[768]{0:T(1024)} %get-tuple-element.95) | copy-start | bytes 9220
  635.4 46.7 %copy-start.44 = (f32[768]{0:T(1024)S(1)}, f32[768]{0:T(1024)}, u32[]{:S(2)}) copy-start(f32[768]{0:T(1024)} %get-tuple-element.98) | copy-start | bytes 9220
  635.4 46.8 %copy-start.11 = (f32[512,768]{1,0:T(8,128)S(1)}, f32[512,768]{1,0:T(8,128)}, u32[]{:S(2)}) copy-start(f32[512,768]{1,0:T(8,128)} %copy-done.10) | copy-start | bytes 4718596
  635.5 47.0 %copy-start.9 = (f32[512,768]{1,0:T(8,128)S(1)}, f32[512,768]{1,0:T(8,128)}, u32[]{:S(2)}) copy-start(f32[512,768]{1,0:T(8,128)} %copy-done.8) | copy-start | bytes 4718596
  635.5 127.1 %all-reduce.3.cloned.1.call-start = ((), (), s32[]{:S(2)}) async-start(), calls=%async_computation.18 | async-start | bytes 3538944 | tf_op jit(solution)/shard_map/psum | solution.py:258
  682.4 47.1 %copy-start.35 = (f32[13,768]{1,0:T(8,128)S(1)}, f32[13,768]{1,0:T(8,128)}, u32[]{:S(2)}) copy-start(f32[13,768]{1,0:T(8,128)} %param.26) | copy-start | bytes 119812
  682.4 47.1 %copy-start.40 = (f32[13,768]{1,0:T(8,128)S(1)}, f32[13,768]{1,0:T(8,128)}, u32[]{:S(2)}) copy-start(f32[13,768]{1,0:T(8,128)} %param.36) | copy-start | bytes 119812
  682.4 47.1 %copy-start.41 = (f32[13,768]{1,0:T(8,128)S(1)}, f32[13,768]{1,0:T(8,128)}, u32[]{:S(2)}) copy-start(f32[13,768]{1,0:T(8,128)} %param.35) | copy-start | bytes 119812
  682.6 47.6 %copy-start.14 = (f32[4,512,192]{1,2,0:T(8,128)S(1)}, f32[4,512,192]{1,2,0:T(8,128)}, u32[]{:S(2)}) copy-start(f32[4,512,192]{1,2,0:T(8,128)} %convert_element_type.233) | copy-start | bytes 4718596
  730.2 32.4 %copy-start.25 = (f32[96,768]{1,0:T(8,128)S(1)}, f32[96,768]{1,0:T(8,128)}, u32[]{:S(2)}) copy-start(f32[96,768]{1,0:T(8,128)} %param.23) | copy-start | bytes 884740
  764.7 3.9 copy-start.22
  764.7 3.9 copy-start.26
  764.7 3.9 copy-start.27
  764.8 3.9 copy-start.33
  768.7 3.2 copy-start.29
  768.7 3.4 copy-start.32
  (11 other events, 19.5 us)
Sparse Core Ops, SparseCore 0:
  10.5 36.6 all-gather.4
  49.7 24.0 all-gather.6
  76.2 38.9 all-gather.8
  117.5 38.9 all-gather.10
  348.0 34.8 reduce-scatter.6
  386.6 53.8 reduce-scatter.8
  444.0 53.8 reduce-scatter.10
  635.6 46.4 reduce-scatter.12
  684.9 77.6 all-reduce.2
where the time goes:
time: 788 us; the launch traced here: 781 us
  waiting for transfers between devices  291 us (37%)
  matrix products  223 us (28%)
  local copies, waits for them, and re-layouts  101 us (13%)
  other arithmetic  80.4 us (10%)
  blocking collectives  43.5 us (6%)
  starting transfers between devices  27.4 us (3%)
  between operations  15.4 us (2%)
    all_to_all x1, waiting for transfers between devices, shards(): lax.all_to_all(pair_back, 'head', split_axis=0, concat_axis=1, tiled=True)  67.2 us
    all_to_all x1, waiting for transfers between devices, shards(): lax.all_to_all(paired, 'head', split_axis=1, concat_axis=0, tiled=True)  64.7 us
    reduce_scatter x1, waiting for transfers between devices, shards(): lax.psum_scatter(local_grads[0].astype(jnp.bfloat16), 'dp', scatter_dimen...  46.4 us
    psum x1, blocking collectives, shards(): vector_total = lax.psum(vector_grad, ('dp', 'head'))  43.5 us
    dot_general x3, matrix products, attend(): jnp.einsum('cik,cjk->cij', block_query, block_key, precision=highest)  38.2 us
    dot_general x3, matrix products, attend(): jnp.einsum('cik,ckd->cid', block_query, before, precision=highest)  37.6 us
    all_gather x1, waiting for transfers between devices, shards(): lax.all_gather(qkv_master.astype(jnp.bfloat16), 'dp', axis=0, tiled=True)  35.1 us
    psum x1, waiting for transfers between devices, shards(): lax.psum(row_parts[0].astype(jnp.bfloat16), 'head').astype(jnp.float32)  26 us
  transfers between devices with their start and end apart: 15, of which 8 were waited for; matrix products, arithmetic and copies ran while one was open for 46% of the time, Pallas kernels for 0%

commit v1 on v0

--- a/solution.py
+++ b/solution.py
@@ -1,8 +1,11 @@
+import functools
 import math
 
 import jax
 import jax.numpy as jnp
 from jax import lax
+from jax.experimental import pallas as pl
+from jax.experimental.pallas import tpu as pltpu
 from jax.sharding import PartitionSpec as P
 
 D = 768
@@ -297,9 +300,637 @@
     )
 
 
+PAIRS = H // 2
+LANES = 2 * HD
+SLABS = PAIRS + 1
+FF_TILE = 512
+ROW_TILE = 128
+MESH = pl.DeviceIdType.MESH
+
+
+def mm(left, right):
+    return jnp.dot(left, right, preferred_element_type=jnp.float32)
+
+
+def mm_cols(left, right):
+    return lax.dot_general(
+        left, right, (((1,), (1,)), ((), ())), preferred_element_type=jnp.float32
+    )
+
+
+def mm_rows(left, right):
+    return lax.dot_general(
+        left, right, (((0,), (0,)), ((), ())), preferred_element_type=jnp.float32
+    )
+
+
+def swap_halves(slab):
+    return pltpu.roll(slab, HD, 1)
+
+
+def low_cast(value):
+    return value.astype(jnp.bfloat16)
+
+
+def gelu_parts(z):
+    x = jnp.abs(z) * (1.0 / math.sqrt(2.0))
+    t = 1.0 / (1.0 + 0.3275911 * x)
+    bell = jnp.exp(-0.5 * z * z)
+    poly = t * (
+        0.254829592
+        + t * (-0.284496736 + t * (1.421413741 + t * (-1.453152027 + t * 1.061405429)))
+    )
+    upper_tail = 0.5 * poly * bell
+    phi = jnp.where(z >= 0, 1.0 - upper_tail, upper_tail)
+    return z * phi, phi + z * (bell * (1.0 / math.sqrt(2.0 * math.pi)))
+
+
+def layer_kernel(
+    n_dp,
+    n_head,
+    n_seq,
+    lens_ref,
+    tok_ref,
+    cot_ref,
+    qkv_f,
+    out_f,
+    up_f,
+    down_f,
+    vec_ref,
+    y_ref,
+    ig_ref,
+    w_qkv,
+    w_out,
+    w_up,
+    w_down,
+    vg_ref,
+    mixed,
+    feat_q,
+    feat_k,
+    val_a,
+    grad_a,
+    num_a,
+    heads,
+    norm_one,
+    rstd_one,
+    hid,
+    hid_low,
+    hid_t,
+    act,
+    gel,
+    two_low,
+    one_low,
+    d_heads,
+    mask,
+    mask_t,
+    cs_ref,
+    rows_ref,
+    keeps,
+    state_own,
+    state_in,
+    back_own,
+    back_in,
+    state_h,
+    back_h,
+    zcol,
+    tok_t,
+    g_send,
+    g_recv,
+    s_send,
+    s_recv,
+):
+    T = tok_ref.shape[0]
+    dp = lax.axis_index("dp")
+    z = lax.axis_index("head")
+    core = dp % 2
+    xx = (dp // 2) % 2
+    yy = dp // 4
+    sib = dp + 1 - 2 * core
+    xn = dp + 2 - 4 * xx
+    yn = dp + 4 - 8 * yy
+    dg = xn + 4 - 8 * yy
+
+    barrier = pltpu.get_barrier_semaphore()
+    for peer in (sib, xn, yn, dg):
+        pl.semaphore_signal(barrier, inc=1, device_id=(peer, z), device_id_type=MESH)
+    for k in range(1, n_head):
+        pl.semaphore_signal(
+            barrier, inc=1, device_id=(dp, (z + k) % n_head), device_id_type=MESH
+        )
+
+    weights = (w_qkv, w_out, w_up, w_down)
+    masters = (qkv_f, out_f, up_f, down_f)
+    depth = tuple(f.shape[0] for f in masters)
+
+    def block(m, who):
+        return pl.ds(pl.multiple_of(who * depth[m], depth[m]), depth[m])
+
+    for m in range(4):
+        weights[m][block(m, dp), :] = low_cast(masters[m][...])
+
+    pl.semaphore_wait(barrier, 4 + n_head - 1)
+
+    def gather_copy(m, kind, who, target):
+        ref = weights[m].at[block(m, who), :]
+        return pltpu.make_async_remote_copy(
+            src_ref=ref,
+            dst_ref=ref,
+            send_sem=g_send.at[m, kind],
+            recv_sem=g_recv.at[m, kind],
+            device_id=(target, z),
+            device_id_type=MESH,
+        )
+
+    def send_own(m):
+        for kind, target in ((1, xn), (2, yn), (3, dg), (0, sib)):
+            gather_copy(m, kind, dp, target).start()
+
+    def hand_over(m):
+        for kind, who in ((1, xn), (2, yn), (3, dg)):
+            gather_copy(m, kind, who, who).wait_recv()
+            gather_copy(m, kind + 3, who, sib).start()
+
+    def all_here(m):
+        for kind in (0, 4, 5, 6):
+            gather_copy(m, kind, dp, sib).wait_recv()
+
+    def all_sent(m):
+        for kind in range(7):
+            gather_copy(m, kind, dp, sib).wait_send()
+
+    for m in range(4):
+        send_own(m)
+
+    lens = [lens_ref[s] for s in range(n_seq)]
+    ends = []
+    total = 0
+    for s in range(n_seq):
+        total = total + ((lens[s] + (SPAN - 1)) // SPAN) * SPAN
+        ends.append(total)
+    starts = [0] + ends[:-1]
+
+    def owner_of(row):
+        found = jnp.zeros_like(row)
+        for s in range(n_seq):
+            found = found + (row >= ends[s]).astype(jnp.int32)
+        return found
+
+    lane = lax.broadcasted_iota(jnp.int32, (T, LANES), 1)
+    row = z * T + lax.broadcasted_iota(jnp.int32, (T, LANES), 0)
+    first = jnp.zeros_like(row)
+    length = jnp.ones_like(row)
+    for s in range(n_seq):
+        inside = (row >= starts[s]) & (row < ends[s])
+        first = jnp.where(inside, starts[s], first)
+        length = jnp.where(inside, lens[s], length)
+    offset = row - first
+    live = (offset < length).astype(jnp.float32)
+    angle = 0.5 * math.pi * offset.astype(jnp.float32) / length.astype(jnp.float32)
+    angle = jnp.where(lane < HD, angle, 0.5 * math.pi - angle)
+    cs_ref[...] = jnp.cos(angle) * live
+    owners = owner_of(row)
+    next_owner = owner_of(jnp.full((1, 1), (z + 1) * T, jnp.int32))
+    last_owner = owner_of(jnp.full((1, 1), z * T - 1, jnp.int32))
+    my_first = owner_of(jnp.full((1, 1), z * T, jnp.int32))
+    my_last = owner_of(jnp.full((1, 1), (z + 1) * T - 1, jnp.int32))
+    rows_ref[...] = live
+    for i, edge in enumerate((next_owner, last_owner, my_first, my_last)):
+        keeps[i] = low_cast((owners == edge).astype(jnp.float32))
+
+    def fill_masks(i, carry):
+        r0 = pl.multiple_of(i * ROW_TILE, ROW_TILE)
+        t_i = r0 + lax.broadcasted_iota(jnp.int32, (ROW_TILE, T), 0)
+        u_i = lax.broadcasted_iota(jnp.int32, (ROW_TILE, T), 1)
+        same = owner_of(t_i + z * T) == owner_of(u_i + z * T)
+        mask[pl.ds(r0, ROW_TILE), :] = (same & (u_i <= t_i)).astype(jnp.float32)
+        mask_t[pl.ds(r0, ROW_TILE), :] = (same & (u_i >= t_i)).astype(jnp.float32)
+        return carry
+
+    lax.fori_loop(0, T // ROW_TILE, fill_masks, 0)
+
+    hand_over(0)
+    all_here(0)
+    for j in range(3):
+        cols = slice(j * D, (j + 1) * D)
+        part = mm(tok_ref[...], w_qkv[:, cols])
+        if j < 2:
+            part = part + vec_ref[6 + j : 7 + j, :]
+        mixed[:, cols] = low_cast(part)
+    hand_over(1)
+
+    half_lane = lax.broadcasted_iota(jnp.int32, (T, LANES), 1)
+    sq_lane = lax.broadcasted_iota(jnp.int32, (LANES, LANES), 1)
+    ones_lane = ((half_lane == HD) | (half_lane == HD + 1)).astype(jnp.float32)
+
+    def softplus(v):
+        return jnp.maximum(v, 0.0) + jnp.log1p(jnp.exp(-jnp.abs(v)))
+
+    def pair_cols(p, part):
+        return pl.ds(pl.multiple_of(part * D + p * LANES, LANES), LANES)
+
+    def split(slab):
+        other = swap_halves(slab)
+        return jnp.where(half_lane < HD, slab, other), jnp.where(half_lane < HD, other, slab)
+
+    def join(left, right):
+        return jnp.where(half_lane < HD, left, swap_halves(right))
+
+    def pack_states(p, low, high, own, n_ones):
+        own[p] = low_cast(jnp.where(sq_lane < HD, low, swap_halves(high)))
+        for side, part in ((0, low), (1, high)):
+            column = part[:, HD : HD + 1]
+            if n_ones == 2:
+                column = column + part[:, HD + 1 : HD + 2]
+            zcol[...] = jnp.where(sq_lane == 2 * p + side, column, zcol[...])
+
+    zcol[...] = jnp.zeros_like(zcol)
+
+    def make_features(p, carry):
+        cs = cs_ref[...]
+        for part, store in ((0, feat_q), (1, feat_k)):
+            low, high = split(softplus(mixed[:, pair_cols(p, part)].astype(jnp.float32)))
+            store[2 * p] = low_cast(low * cs)
+            store[2 * p + 1] = low_cast(high * cs)
+        v_pair = mixed[:, pair_cols(p, 2)].astype(jnp.float32)
+        val_a[2 * p] = low_cast(jnp.where(half_lane < HD, v_pair, ones_lane))
+        val_a[2 * p + 1] = low_cast(jnp.where(half_lane < HD, swap_halves(v_pair), ones_lane))
+        keep = keeps[0]
+        low = mm_rows(feat_k[2 * p] * keep, val_a[2 * p])
+        high = mm_rows(feat_k[2 * p + 1] * keep, val_a[2 * p + 1])
+        pack_states(p, low, high, state_own, 1)
+        return carry
+
+    lax.fori_loop(0, PAIRS, make_features, 0)
+    state_own[PAIRS] = low_cast(zcol[...])
+
+    def exchange(which, own, landed, k):
+        return pltpu.make_async_remote_copy(
+            src_ref=own,
+            dst_ref=landed.at[z],
+            send_sem=s_send.at[which, k],
+            recv_sem=s_recv.at[which, k],
+            device_id=(dp, (z + k) % n_head),
+            device_id_type=MESH,
+        )
+
+    for k in range(1, n_head):
+        exchange(0, state_own, state_in, k).start()
+
+    def local_attend(h, carry):
+        scores = mm_cols(feat_q[h], feat_k[h]) * mask[...]
+        num_a[h] = mm(low_cast(scores), val_a[h])
+        return carry
+
+    lax.fori_loop(0, H, local_attend, 0)
+    hand_over(2)
+
+    def gather_states(which, own, landed, weight_of, out, n_ones):
+        for k in range(1, n_head):
+            exchange(which, own, landed, k).wait_recv()
+
+        def unpack(p, carry):
+            packed = jnp.zeros((LANES, LANES), jnp.float32)
+            ends_col = jnp.zeros((LANES, LANES), jnp.float32)
+            for k in range(1, n_head):
+                src = (z + n_head - k) % n_head
+                weight = weight_of(src)
+                packed = packed + weight * landed[src, p].astype(jnp.float32)
+                ends_col = ends_col + weight * landed[src, PAIRS].astype(jnp.float32)
+            for side in (0, 1):
+                column = jnp.sum(
+                    jnp.where(sq_lane == 2 * p + side, ends_col, 0.0), axis=1, keepdims=True
+                )
+                slab = packed if side == 0 else swap_halves(packed)
+                wide = (sq_lane >= HD) & (sq_lane < HD + n_ones)
+                out[2 * p + side] = low_cast(
+                    jnp.where(sq_lane < HD, slab, jnp.where(wide, column, 0.0))
+                )
+            return carry
+
+        lax.fori_loop(0, PAIRS, unpack, 0)
+
+    def forward_weight(src):
+        edge = owner_of(jnp.full((1, 1), (src + 1) * T, jnp.int32))
+        return ((edge == my_first) & (src < z)).astype(jnp.float32)
+
+    def backward_weight(src):
+        edge = owner_of(jnp.full((1, 1), src * T - 1, jnp.int32))
+        return ((edge == my_last) & (src > z)).astype(jnp.float32)
+
+    gather_states(0, state_own, state_in, forward_weight, state_h, 2)
+
+    def finish_heads(p, carry):
+        att = []
+        for side in (0, 1):
+            h = 2 * p + side
+            total = num_a[h] + mm(feat_q[h] * keeps[2], state_h[h])
+            den = total[:, HD : HD + 1] + (1.0 - rows_ref[...])
+            inverse = 1.0 / den
+            got = total * inverse
+            num_a[h] = jnp.where(half_lane < HD, got, inverse)
+            att.append(got)
+        joined = join(att[0], att[1])
+        shift = vec_ref[8:9, pl.ds(pl.multiple_of(p * LANES, LANES), LANES)]
+        heads[:, pair_cols(p, 0)] = low_cast(joined + shift * rows_ref[...])
+        return carry
+
+    lax.fori_loop(0, PAIRS, finish_heads, 0)
+
+    all_here(1)
+
+    def first_norm(i, carry):
+        r = pl.ds(pl.multiple_of(i * ROW_TILE, ROW_TILE), ROW_TILE)
+        residual = tok_ref[r, :].astype(jnp.float32) + (mm(heads[r, :], w_out[...]) + vec_ref[4:5, :])
+        center = residual - jnp.mean(residual, axis=-1, keepdims=True)
+        rstd = lax.rsqrt(jnp.mean(center * center, axis=-1, keepdims=True) + norm_epsilon)
+        normed = center * rstd
+        norm_one[r, :] = normed
+        rstd_one[r, :] = jnp.broadcast_to(rstd, (ROW_TILE, LANES))
+        hidden = normed * vec_ref[0:1, :] + vec_ref[1:2, :]
+        hid[r, :] = hidden
+        hid_low[r, :] = low_cast(hidden)
+        return carry
+
+    lax.fori_loop(0, T // ROW_TILE, first_norm, 0)
+
+    hand_over(3)
+    all_here(2)
+
+    def ff_up(j, carry):
+        cols = pl.ds(pl.multiple_of(j * FF_TILE, FF_TILE), FF_TILE)
+        upper = mm(hid_low[...], w_up[:, cols]) + vg_ref[0:1, cols]
+        value, slope = gelu_parts(upper)
+        act[:, cols] = low_cast(value)
+        gel[:, cols] = low_cast(slope)
+        return carry
+
+    for j in range(4):
+        vg_ref[0:1, j * D : (j + 1) * D] = vec_ref[9 + j : 10 + j, :]
+    lax.fori_loop(0, FF // FF_TILE, ff_up, 0)
+
+    all_here(3)
+
+    def row_sum(value):
+        return jnp.sum(value, axis=0, keepdims=True)
+
+    def second_norm(i, sums):
+        r = pl.ds(pl.multiple_of(i * ROW_TILE, ROW_TILE), ROW_TILE)
+        residual = hid[r, :] + (mm(act[r, :], w_down[...]) + vec_ref[5:6, :])
+        center = residual - jnp.mean(residual, axis=-1, keepdims=True)
+        rstd = lax.rsqrt(jnp.mean(center * center, axis=-1, keepdims=True) + norm_epsilon)
+        normed = center * rstd
+        y_ref[r, :] = low_cast(normed * vec_ref[2:3, :] + vec_ref[3:4, :])
+        dy = cot_ref[r, :]
+        e = dy * vec_ref[2:3, :]
+        d_two = rstd * (
+            e
+            - jnp.mean(e, axis=-1, keepdims=True)
+            - normed * jnp.mean(e * normed, axis=-1, keepdims=True)
+        )
+        hid[r, :] = d_two
+        two_low[r, :] = low_cast(d_two)
+        return sums[0] + row_sum(dy * normed), sums[1] + row_sum(dy), sums[2] + row_sum(d_two)
+
+    zero_row = jnp.zeros((1, D), jnp.float32)
+    gain_two, shift_two, bias_down = lax.fori_loop(
+        0, T // ROW_TILE, second_norm, (zero_row, zero_row, zero_row)
+    )
+
+    def ff_back(j, carry):
+        cols = pl.ds(pl.multiple_of(j * FF_TILE, FF_TILE), FF_TILE)
+        d_upper = mm_cols(two_low[...], w_down[cols, :]) * gel[:, cols].astype(jnp.float32)
+        gel[:, cols] = low_cast(d_upper)
+        vg_ref[1:2, cols] = row_sum(d_upper)
+        return carry
+
+    lax.fori_loop(0, FF // FF_TILE, ff_back, 0)
+    all_sent(3)
+
+    def grad_down(j, carry):
+        cols = pl.ds(pl.multiple_of(j * FF_TILE, FF_TILE), FF_TILE)
+        w_down[cols, :] = low_cast(mm_rows(act[:, cols], two_low[...]))
+        return carry
+
+    lax.fori_loop(0, FF // FF_TILE, grad_down, 0)
+
+    def norm_back(i, sums):
+        r = pl.ds(pl.multiple_of(i * ROW_TILE, ROW_TILE), ROW_TILE)
+        dy = hid[r, :] + mm_cols(gel[r, :], w_up[...])
+        normed = norm_one[r, :]
+        rstd = rstd_one[r, 0:1]
+        e = dy * vec_ref[0:1, :]
+        d_one = rstd * (
+            e
+            - jnp.mean(e, axis=-1, keepdims=True)
+            - normed * jnp.mean(e * normed, axis=-1, keepdims=True)
+        )
+        ig_ref[r, :] = d_one
+        one_low[r, :] = low_cast(d_one)
+        return sums[0] + row_sum(dy * normed), sums[1] + row_sum(dy), sums[2] + row_sum(d_one)
+
+    gain_one, shift_one, bias_out = lax.fori_loop(
+        0, T // ROW_TILE, norm_back, (zero_row, zero_row, zero_row)
+    )
+    all_sent(2)
+    hid_t[...] = hid_low[...].T
+
+    def grad_up(j, carry):
+        cols = pl.ds(pl.multiple_of(j * FF_TILE, FF_TILE), FF_TILE)
+        w_up[:, cols] = low_cast(mm(hid_t[...], gel[:, cols]))
+        return carry
+
+    lax.fori_loop(0, FF // FF_TILE, grad_up, 0)
+
+    d_heads[...] = low_cast(mm_cols(one_low[...], w_out[...]))
+    all_sent(1)
+    w_out[...] = low_cast(mm_rows(heads[...], one_low[...]))
+
+    zcol[...] = jnp.zeros_like(zcol)
+
+    def back_states(p, carry):
+        g_pair = d_heads[:, pair_cols(p, 0)].astype(jnp.float32)
+        parts = []
+        for side in (0, 1):
+            h = 2 * p + side
+            saved = num_a[h]
+            g = g_pair if side == 0 else swap_halves(g_pair)
+            gn = jnp.where(half_lane < HD, g * swap_halves(saved), 0.0)
+            gd = -jnp.sum(gn * saved, axis=1, keepdims=True)
+            gd_high = low_cast(gd).astype(jnp.float32)
+            gn = jnp.where(
+                half_lane == HD, gd_high, jnp.where(half_lane == HD + 1, gd - gd_high, gn)
+            )
+            grad_a[h] = low_cast(gn)
+            parts.append(mm_rows(feat_q[h] * keeps[1], grad_a[h]))
+        pack_states(p, parts[0], parts[1], back_own, 2)
+        return carry
+
+    lax.fori_loop(0, PAIRS, back_states, 0)
+    back_own[PAIRS] = low_cast(zcol[...])
+    for k in range(1, n_head):
+        exchange(1, back_own, back_in, k).start()
+    gather_states(1, back_own, back_in, backward_weight, back_h, 1)
+
+    def mix_back(p, carry):
+        cs = cs_ref[...]
+        got = []
+        for side in (0, 1):
+            h = 2 * p + side
+            fq, fk, va, ga = feat_q[h], feat_k[h], val_a[h], grad_a[h]
+            d_scores = low_cast(mm_cols(ga, va) * mask[...])
+            dq = mm(d_scores, fk) + mm_cols(ga * keeps[2], state_h[h])
+            d_scores_t = low_cast(mm_cols(va, ga) * mask_t[...])
+            dk = mm(d_scores_t, fq) + mm_cols(va * keeps[3], back_h[h])
+            scores_t = low_cast(mm_cols(fk, fq) * mask_t[...])
+            dv = mm(scores_t, ga) + mm(fk * keeps[3], back_h[h])
+            dq = dq * cs
+            dk = dk * cs
+            got.append((dq + swap_halves(dq), dk + swap_halves(dk), dv))
+        for part in (0, 1):
+            value = mixed[:, pair_cols(p, part)].astype(jnp.float32)
+            e = jnp.exp(-jnp.abs(value))
+            sigma = jnp.where(value >= 0, 1.0, e) / (1.0 + e)
+            d_part = sigma * jnp.where(half_lane < HD, got[0][part], got[1][part])
+            mixed[:, pair_cols(p, part)] = low_cast(d_part)
+            vg_ref[2:3, pair_cols(p, part)] = row_sum(d_part)
+        d_part = join(got[0][2], got[1][2])
+        mixed[:, pair_cols(p, 2)] = low_cast(d_part)
+        vg_ref[2:3, pair_cols(p, 2)] = row_sum(d_part)
+        return carry
+
+    lax.fori_loop(0, PAIRS, mix_back, 0)
+
+    for j in range(3):
+        cols = slice(j * D, (j + 1) * D)
+        ig_ref[...] += mm_cols(mixed[:, cols], w_qkv[:, cols])
+    all_sent(0)
+    tok_t[...] = tok_ref[...].T
+    for j in range(3):
+        cols = slice(j * D, (j + 1) * D)
+        w_qkv[:, cols] = low_cast(mm(tok_t[...], mixed[:, cols]))
+    for k in range(1, n_head):
+        exchange(0, state_own, state_in, k).wait_send()
+        exchange(1, back_own, back_in, k).wait_send()
+
+    ups = [vg_ref[1:2, j * D : (j + 1) * D] for j in range(4)]
+    mix = [vg_ref[2:3, j * D : (j + 1) * D] for j in range(3)]
+    vg_rows = [gain_one, shift_one, gain_two, shift_two, bias_out, bias_down] + mix + ups
+    for i, value in enumerate(vg_rows):
+        vg_ref[i : i + 1, 0:D] = value
+
+
+def fits(mesh):
+    return mesh.shape["dp"] == 8
+
+
+def fused_layer(n_dp, n_head, lengths, tokens, cotangent, masters, vector_master):
+    T = tokens.shape[0]
+    bf, f32 = jnp.bfloat16, jnp.float32
+    vm = pl.BlockSpec(memory_space=pltpu.VMEM)
+    out_shape = (
+        jax.ShapeDtypeStruct((T, D), bf),
+        jax.ShapeDtypeStruct((T, D), f32),
+        jax.ShapeDtypeStruct((D, 3 * D), bf),
+        jax.ShapeDtypeStruct((D, D), bf),
+        jax.ShapeDtypeStruct((D, FF), bf),
+        jax.ShapeDtypeStruct((FF, D), bf),
+        jax.ShapeDtypeStruct((16, FF), f32),
+    )
+    V = pltpu.VMEM
+    scratch = [
+        V((T, 3 * D), bf),
+        V((H, T, LANES), bf),
+        V((H, T, LANES), bf),
+        V((H, T, LANES), bf),
+        V((H, T, LANES), bf),
+        V((H, T, LANES), f32),
+        V((T, D), bf),
+        V((T, D), f32),
+        V((T, LANES), f32),
+        V((T, D), f32),
+        V((T, D), bf),
+        V((D, T), bf),
+        V((T, FF), bf),
+        V((T, FF), bf),
+        V((T, D), bf),
+        V((T, D), bf),
+        V((T, D), bf),
+        V((T, T), f32),
+        V((T, T), f32),
+        V((T, LANES), f32),
+        V((T, LANES), f32),
+        V((4, T, LANES), bf),
+        V((SLABS, LANES, LANES), bf),
+        V((n_head, SLABS, LANES, LANES), bf),
+        V((SLABS, LANES, LANES), bf),
+        V((n_head, SLABS, LANES, LANES), bf),
+        V((H, LANES, LANES), bf),
+        V((H, LANES, LANES), bf),
+        V((LANES, LANES), f32),
+        V((D, T), bf),
+        pltpu.SemaphoreType.DMA((4, 7)),
+        pltpu.SemaphoreType.DMA((4, 7)),
+        pltpu.SemaphoreType.DMA((2, n_head)),
+        pltpu.SemaphoreType.DMA((2, n_head)),
+    ]
+    return pl.pallas_call(
+        functools.partial(layer_kernel, n_dp, n_head, lengths.shape[0]),
+        out_shape=out_shape,
+        in_specs=[pl.BlockSpec(memory_space=pltpu.SMEM)] + [vm] * 7,
+        out_specs=[vm] * 7,
+        scratch_shapes=scratch,
+        compiler_params=pltpu.CompilerParams(
+            collective_id=0, has_side_effects=True, vmem_limit_bytes=62 * 1024 * 1024
+        ),
+        name="layer",
+    )(lengths, tokens, cotangent, *masters, vector_master)
+
+
+def fused_shards(
+    tokens,
+    cotangent,
+    lengths,
+    qkv_master,
+    out_master,
+    up_master,
+    down_master,
+    vector_master,
+    qkv_first,
+    qkv_second,
+    out_first,
+    out_second,
+    up_first,
+    up_second,
+    down_first,
+    down_second,
+    vector_first,
+    vector_second,
+):
+    n_dp, n_head = lax.axis_size("dp"), lax.axis_size("head")
+    masters = (qkv_master, out_master, up_master, down_master)
+    output, input_grad, *grads, vector_grad = fused_layer(
+        n_dp, n_head, lengths, tokens, cotangent, masters, vector_master
+    )
+    parts = [lax.psum_scatter(g, "dp", scatter_dimension=0, tiled=True) for g in grads]
+    reduced = [g.astype(jnp.float32) for g in lax.psum(tuple(parts), "head")]
+    vector_total = lax.psum(vector_grad[:13, :D], ("dp", "head"))
+    rates = (1.0 / math.sqrt(D), 1.0 / math.sqrt(OUT_FAN), 1.0 / math.sqrt(D), 1.0 / math.sqrt(FF))
+    firsts = (qkv_first, out_first, up_first, down_first)
+    seconds = (qkv_second, out_second, up_second, down_second)
+    news = []
+    for i in range(4):
+        news.extend(
+            adam_update(masters[i], firsts[i], seconds[i], reduced[i], rates[i], weight_decay)
+        )
+    vector_new = adam_update(
+        vector_master, vector_first, vector_second, vector_total, vector_rate, 0.0
+    )
+    return (output, input_grad, *news, *vector_new)
+
+
 def solution(mesh):
     return jax.shard_map(
-        shards,
+        fused_shards if fits(mesh) else shards,
         mesh=mesh,
         in_specs=(
             P(("dp", "head"), None),

time: 788 us -> 481 us (0.61)
  matrix products: 223 us -> 0 us
  Pallas kernels: 0 us -> 168 us
  local copies, waits for them, and re-layouts: 101 us -> 4.85 us
  other arithmetic: 80.4 us -> 10.5 us
  waiting for transfers between devices: 291 us -> 240 us
  starting transfers between devices: 27.4 us -> 0.19 us
    dot_general x30 -> x0, matrix products: 223 us -> none  [the longest x3 38.2 us: attend(): jnp.einsum('cik,cjk->cij', block_query, block_key, precision=highest)]
    all_to_all x6 -> x0, waiting for transfers between devices: 183 us -> none  [the longest x1 67.2 us: shards(): lax.all_to_all(pair_back, 'head', split_axis=0, concat_axis=1, tiled=True)]
    pallas_call x0 -> x1, Pallas kernels: none -> 168 us  [fused_layer(): pl.pallas_call(functools.partial(layer_kernel, n_dp, n_head, lengths.shap...]
    reduce_scatter x4, waiting for transfers between devices: 46.5 us -> 204 us  [fused_shards(): lax.psum_scatter(g, 'dp', scatter_dimension=0, tiled=True)]
    all_gather x4 -> x0, waiting for transfers between devices: 35.1 us -> none  [the longest x1 35.1 us: shards(): lax.all_gather(qkv_master.astype(jnp.bfloat16), 'dp', axis=0, tiled=True)]
    convert_element_type x9 -> x0, local copies, waits for them, and re-layouts: 29.2 us -> none  [the longest x2 15.1 us: shards(): paired_in.reshape(group_rows, item_count, 2, HD).astype(jnp.float32)]
    all_to_all x6 -> x0, starting transfers between devices: 26.4 us -> none  [the longest x1 5.04 us: shards(): lax.all_to_all(pair_back, 'head', split_axis=0, concat_axis=1, tiled=True)]
    concatenate x6 -> x0, local copies, waits for them, and re-layouts: 23.4 us -> none  [the longest x2 11.6 us: attend(): jnp.concatenate([soft_query * cosine[:, None], soft_query * sine_part[:,...]
  transfers between devices with their start and end apart: 15 -> 5, of which waited for: 8 -> 5; matrix products, arithmetic and copies ran while one was open for 46% -> 1% of each run, Pallas kernels for 0% -> 0%
where the time goes in v1:
time: 481 us; the launch traced here: 480 us
  waiting for transfers between devices  240 us (50%)
  Pallas kernels  168 us (35%)
  blocking collectives  43.3 us (9%)
  between operations  13.9 us (3%)
  other arithmetic  10.5 us (2%)
  local copies, waits for them, and re-layouts  4.85 us (1%)
    reduce_scatter x4, waiting for transfers between devices, fused_shards(): lax.psum_scatter(g, 'dp', scatter_dimension=0, tiled=True)  204 us
    pallas_call x1, Pallas kernels, fused_layer(): pl.pallas_call(functools.partial(layer_kernel, n_dp, n_head, lengths.shap...  168 us
    psum x1, blocking collectives, fused_shards(): vector_total = lax.psum(vector_grad[:13, :D], ('dp', 'head'))  43.3 us
    psum x1, waiting for transfers between devices, fused_shards(): reduced = [g.astype(jnp.float32) for g in lax.psum(tuple(parts), 'head')]  34.1 us
    sub x5, other arithmetic, adam_update(): master - rate * (first_hat / (jnp.sqrt(second_hat) + adam_epsilon) + deca...  10.5 us
  transfers between devices with their start and end apart: 5, of which 5 were waited for; matrix products, arithmetic and copies ran while one was open for 1% of the time, Pallas kernels for 0%

profile of v1, /device:TPU:0, one launch (start us, length us, event | category | flops | bytes accessed | tf_op | source)
XLA Modules:
  0.0 480.4 jit_solution(18000289438196357198)
XLA Ops:
  7.2 0.0 reduce-scatter.7.cloned.1.call-start
  7.2 167.7 %layer.1 = (bf16[512,768]{1,0:T(8,128)(2,1)}, f32[512,768]{1,0:T(8,128)}, bf16[768,2304]{1,0:T(8,128)(2,1)}, bf16[768,768]{1,0:T(8,128)(2,1)}, bf16[768,3072]{1,...) custom-call(s32[2]{0:T(128)} %lens_ref.1, bf16[512,768]{1,0:T(8,128)(2,1)} %tok_ref.1, ...), custom_call_target="tpu_custom_call" | custom-call | tf_op jit(solution)/shard_map/layer/pallas_call | solution.py:876
  175.0 0.0 reduce-scatter.7.cloned.1.call-update
  175.0 0.0 reduce-scatter.5.cloned.1.call-start
  175.1 0.7 reduce-scatter.5.cloned.1.call-update
  175.8 0.0 reduce-scatter.11.cloned.1.call-start
  175.8 0.7 reduce-scatter.11.cloned.1.call-update
  176.5 0.0 reduce-scatter.9.cloned.1.call-start
  176.5 0.0 copy-start.5
  176.5 0.0 copy-start.6
  176.6 0.5 reduce-scatter.9.cloned.1.call-update
  177.1 0.0 copy-start
  177.1 0.0 all-reduce.3.cloned.1.call-start
  177.1 36.8 %reduce-scatter.7.cloned.1.call-done = bf16[96,768]{1,0:T(8,128)(2,1)} async-done(((bf16[768,768]{1,0:T(8,128)(2,1)}), bf16[96,768]{1,0:T(8,128)(2,1)}) %reduce-scatter.7.cloned.1.call-update) | async-done | bytes 147472 | tf_op jit(solution)/shard_map/reduce_scatter | solution.py:914
  213.9 52.0 %reduce-scatter.5.cloned.1.call-done = bf16[96,2304]{1,0:T(8,128)(2,1)} async-done(((bf16[768,2304]{1,0:T(8,128)(2,1)}), bf16[96,2304]{1,0:T(8,128)(2,1)}) %reduce-scatter.5.cloned.1.call-update) | async-done | bytes 442384 | tf_op jit(solution)/shard_map/reduce_scatter | solution.py:914
  266.0 57.7 %reduce-scatter.11.cloned.1.call-done = bf16[384,768]{1,0:T(8,128)(2,1)} async-done(((bf16[3072,768]{1,0:T(8,128)(2,1)}), bf16[384,768]{1,0:T(8,128)(2,1)}) %reduce-scatter.11.cloned.1.call-update) | async-done | bytes 589840 | tf_op jit(solution)/shard_map/reduce_scatter | solution.py:914
  323.7 57.2 %reduce-scatter.9.cloned.1.call-done = bf16[96,3072]{1,0:T(8,128)(2,1)} async-done(((bf16[768,3072]{1,0:T(8,128)(2,1)}), bf16[96,3072]{1,0:T(8,128)(2,1)}) %reduce-scatter.9.cloned.1.call-update) | async-done | bytes 589840 | tf_op jit(solution)/shard_map/reduce_scatter | solution.py:914
  380.9 0.0 all-reduce.3.cloned.1.call-update
  381.0 1.4 slice.3
  382.4 43.3 %psum.39 = f32[13,768]{1,0:T(8,128)} all-reduce(f32[13,768]{1,0:T(8,128)} %slice.3), channel_id=1, replica_groups=mesh['dp'=8,'head'=4] {'dp','head'}, use_global_device_ids=true, to_apply=%region_8.0 | all-reduce | flops 9984 | bytes 79872 | tf_op jit(solution)/shard_map/psum | solution.py:916
  425.6 1.5 multiply_subtract_fusion.3
  427.2 34.1 %all-reduce.3.cloned.1.call-done = (bf16[96,2304]{1,0:T(8,128)(2,1)}, bf16[96,768]{1,0:T(8,128)(2,1)}, bf16[96,3072]{1,0:T(8,128)(2,1)}, bf16[384,768]{1,0:T(8,128)(2,1)}) async-done(((bf16[96,2304]{1,0:T(8,128)(2,1)}, bf16[96,768]{1,0:T(8,128)(2,1)}, bf16[96,3072]{1,0:T(8,128)(2,1)}, bf16[384,768]{1,0:T(8,128)(2,1)}), (bf16[96,2304]{1,0:T(8,128)(2,1)}, bf16[96,768]{1,0:T(8,128)(2,1)}, ...) | async-done | bytes 1769488 | tf_op jit(solution)/shard_map/psum | solution.py:915
  461.3 0.0 copy-done.5
  461.3 0.0 copy-done.6
  461.3 0.0 copy-done
  461.3 0.0 copy-start.1
  461.3 0.0 copy-start.7
  461.3 0.0 copy-start.8
  461.3 0.0 copy-start.12
  461.4 3.6 multiply_subtract_fusion.1
  465.0 0.0 copy-done.1
  465.0 0.0 copy-done.7
  465.0 0.0 copy-done.8
  465.0 0.0 copy-done.12
  465.0 0.0 copy-start.2
  465.0 0.0 copy-start.9
  465.0 0.0 copy-start.10
  465.0 0.0 copy-start.13
  465.0 2.4 multiply_subtract_fusion
  467.4 0.0 copy-done.2
  467.4 0.0 copy-done.9
  467.4 0.0 copy-done.10
  467.5 0.4 copy-done.13
  467.9 0.0 copy-start.4
  467.9 0.0 copy-start.14
  467.9 0.0 copy-start.15
  467.9 0.0 copy-start.16
  467.9 1.9 multiply_subtract_fusion.2
  469.9 0.0 copy-start.11
  469.9 0.0 copy-done.4
  469.9 0.0 copy-done.14
  469.9 0.0 copy-done.15
  469.9 0.0 copy-done.16
  469.9 1.0 add_subtract_fusion
  470.9 0.0 copy-start.3
  470.9 0.3 copy-done.11
  471.3 0.9 copy.41
  472.1 0.5 copy-done.3
  472.7 1.1 copy.42
Async XLA Ops:
  7.2 206.7 %reduce-scatter.7.cloned.1.call-start = ((), (), s32[]{:S(2)}) async-start(), calls=%async_computation.5 | async-start | bytes 1327104 | tf_op jit(solution)/shard_map/reduce_scatter | solution.py:914
  175.0 91.0 %reduce-scatter.5.cloned.1.call-start = ((), (), s32[]{:S(2)}) async-start(), calls=%async_computation.4 | async-start | bytes 3981312 | tf_op jit(solution)/shard_map/reduce_scatter | solution.py:914
  175.8 148.0 %reduce-scatter.11.cloned.1.call-start = ((), (), s32[]{:S(2)}) async-start(), calls=%async_computation.7 | async-start | bytes 5308416 | tf_op jit(solution)/shard_map/reduce_scatter | solution.py:914
  176.5 204.5 %reduce-scatter.9.cloned.1.call-start = ((), (), s32[]{:S(2)}) async-start(), calls=%async_computation.6 | async-start | bytes 5308416 | tf_op jit(solution)/shard_map/reduce_scatter | solution.py:914
  176.5 284.8 %copy-start.5 = (f32[96,3072]{1,0:T(8,128)S(1)}, f32[96,3072]{1,0:T(8,128)}, u32[]{:S(2)}) copy-start(f32[96,3072]{1,0:T(8,128)} %param.31) | copy-start | bytes 3538948
  176.5 284.8 %copy-start.6 = (f32[96,3072]{1,0:T(8,128)S(1)}, f32[96,3072]{1,0:T(8,128)}, u32[]{:S(2)}) copy-start(f32[96,3072]{1,0:T(8,128)} %param.30) | copy-start | bytes 3538948
  177.1 284.2 %copy-start = (f32[96,3072]{1,0:T(8,128)S(1)}, f32[96,3072]{1,0:T(8,128)}, u32[]{:S(2)}) copy-start(f32[96,3072]{1,0:T(8,128)} %up_f.1) | copy-start | bytes 3538948
  177.1 284.2 %all-reduce.3.cloned.1.call-start = ((), (), s32[]{:S(2)}) async-start(), calls=%async_computation.8 | async-start | bytes 3538944 | tf_op jit(solution)/shard_map/psum | solution.py:915
  461.3 3.6 copy-start.1
  461.3 3.6 copy-start.7
  461.3 3.6 copy-start.8
  461.3 3.6 copy-start.12
  465.0 2.5 copy-start.2
  465.0 2.5 copy-start.9
  465.0 2.5 copy-start.10
  465.0 2.9 copy-start.13
  467.9 2.0 copy-start.4
  467.9 2.0 copy-start.14
  467.9 2.0 copy-start.15
  467.9 2.0 copy-start.16
  469.9 1.4 copy-start.11
  470.9 1.8 copy-start.3
Sparse Core Ops, SparseCore 0:
  175.1 38.7 reduce-scatter.6
  217.8 48.1 reduce-scatter.4
  269.8 53.8 reduce-scatter.10
  327.0 53.8 reduce-scatter.8
  383.6 77.6 all-reduce.2
